TPU v7x, 256 devices: a whole 4x4x8 slice. The times are simulated.
256 devices in a mesh: fsdp: 32 (over z_hi, x, core), tp: 8 (over y, z_lo).
Axes of the slice: x: 4, y: 4, z: 8 (z_hi: 4, z_lo: 2; z = z_hi * 2 + z_lo), core: 2. Of those that a mesh axis runs over, the one named last changes fastest.
Arguments:
- activations: bfloat16 [8192, 8192], P('fsdp'), may hold values from -6 to 6
- grad_output: bfloat16 [8192, 28672], P('fsdp', 'tp'), may hold values from -0.1875 to 0.1875
- projector: bfloat16 [8192, 1024], P('fsdp'), may hold values from -0.125 to 0.125
- first_moment: float32 [1024, 28672], P('fsdp', 'tp'), may hold values from -0.625 to 0.625
- second_moment: float32 [1024, 28672], P('fsdp', 'tp'), may hold values from 0.01 to 0.5
Outputs:
- new_first: float32 [1024, 28672], P('fsdp', 'tp')
- new_second: float32 [1024, 28672], P('fsdp', 'tp')
- weight_update: bfloat16 [8192, 28672], P('fsdp', 'tp')
All inputs are finite; a program needn't handle non-finite values.
Results may differ from a plain program's by a relative error of at most 0.0059.
Values may be sent and summed in bfloat16 or wider, within the bound.
No kernel may reach another device: no remote copies, remote signals or barrier semaphores. Data moves between devices by JAX's collectives and lax.ppermute only.
A program may use at most 64 MiB of HBM per device.

v0:
```python
import jax
import jax.numpy as jnp
from jax import lax
from jax.sharding import PartitionSpec as P

first_fix = 0.9999734386011124
second_fix = 0.6339676587267705


def body(activations, grad_output, projector, first_moment, second_moment):
    rank_width = projector.shape[1]
    tp_count = lax.axis_size("tp")
    tp_place = lax.axis_index("tp")
    column_count = rank_width // tp_count
    spread = lax.all_to_all(activations, "fsdp", split_axis=1, concat_axis=0, tiled=True)
    proj_block = lax.dynamic_slice_in_dim(projector, tp_place * column_count, column_count, 1)
    partial_coords = lax.psum_scatter(
        jnp.dot(spread, proj_block, preferred_element_type=jnp.float32),
        "fsdp",
        scatter_dimension=0,
        tiled=True,
    ).astype(jnp.bfloat16)
    coords = lax.all_gather(partial_coords, "tp", axis=1, tiled=True)
    lowrank = lax.psum_scatter(
        lax.dot_general(
            coords, grad_output, (((0,), (0,)), ((), ())), preferred_element_type=jnp.float32
        ),
        "fsdp",
        scatter_dimension=0,
        tiled=True,
    )
    new_first = 0.9 * first_moment + 0.1 * lowrank
    new_second = 0.99 * second_moment + 0.01 * lowrank * lowrank
    direction = (new_first / first_fix / (jnp.sqrt(new_second / second_fix) + 1e-08)).astype(
        jnp.bfloat16
    )
    summed = jnp.dot(
        projector,
        lax.all_gather(direction, "fsdp", axis=0, tiled=True),
        preferred_element_type=jnp.float32,
    )
    return (new_first, new_second, summed.astype(jnp.bfloat16))


def solution(mesh):
    return jax.shard_map(
        body,
        mesh=mesh,
        in_specs=(
            P("fsdp", None),
            P("fsdp", "tp"),
            P("fsdp", None),
            P("fsdp", "tp"),
            P("fsdp", "tp"),
        ),
        out_specs=(P("fsdp", "tp"), P("fsdp", "tp"), P("fsdp", "tp")),
        check_vma=False,
    )
```

profile of v0, /device:TPU:1, one launch (start us, length us, event | category | flops | bytes accessed | tf_op | source)
XLA Modules:
  0.0 510.6 jit_solution(12364093431494261949)
XLA Ops:
  7.2 0.0 copy-start
  7.2 6.6 %copy.10 = bf16[256,8192]{0,1:T(8,128)(2,1)} copy(bf16[256,8192]{1,0:T(8,128)(2,1)} %param.5) | data formatting | bytes 8388608 | tf_op args[0]
  13.8 12.6 %all-to-all-start = ((bf16[256,32,256]{0,2,1:T(8,128)(2,1)}), bf16[256,32,256]{0,2,1:T(8,128)(2,1)}, u32[]{:S(2)}, u32[]{:S(2)}) async-start(bf16[256,32,256]{0,2,1:T(8,128)(2,1)} %bitcast.12), calls=%async_computation | async-start | bytes 8388608 | tf_op jit(solution)/shard_map/all_to_all | solution.py:15
  26.4 0.0 reduce-scatter.3.cloned.1.call-start
  26.5 95.8 %all-to-all-done = bf16[256,32,256]{0,2,1:T(8,128)(2,1)} async-done(((bf16[256,32,256]{0,2,1:T(8,128)(2,1)}), bf16[256,32,256]{0,2,1:T(8,128)(2,1)}, u32[]{:S(2)}, u32[]{:S(2)}) %all-to-all-start) | async-done | bytes 4194336 | tf_op jit(solution)/shard_map/all_to_all | solution.py:15
  122.3 0.0 copy-start.3
  122.3 6.5 %copy.11 = bf16[32,256,256]{2,1,0:T(8,128)(2,1)} copy(bf16[32,256,256]{1,2,0:T(8,128)(2,1)} %bitcast.1) | data formatting | bytes 8388608 | tf_op jit(solution)/shard_map/all_to_all | solution.py:15
  128.8 0.0 copy-done.3
  128.8 5.6 %convolution_bitcast_fusion = f32[8192,128]{0,1:T(8,128)} fusion(bf16[8192,256]{1,0:T(8,128)(2,1)} %bitcast.13, bf16[256,1024]{1,0:T(8,128)(2,1)S(1)} %copy-done.3, s32[]{:T(128)S(6)} %select_n.3), kind=kOutput, calls=%fused_computation | convolution fusion | flops 536870912 | bytes 8454148 | tf_op jit(solution)/shard_map/dot_general | solution.py:18
  134.4 0.0 reduce-scatter.3.cloned.1.call-update
  134.5 0.0 reduce-scatter.5.cloned.1.call-start
  134.5 94.8 %reduce-scatter.3.cloned.1.call-done = f32[256,128]{0,1:T(8,128)} async-done(((f32[8192,128]{0,1:T(8,128)}), f32[256,128]{0,1:T(8,128)}) %reduce-scatter.3.cloned.1.call-update) | async-done | bytes 131088 | tf_op jit(solution)/shard_map/reduce_scatter | solution.py:17
  229.3 0.9 convert_element_type.12
  230.2 24.1 %all_gather.6 = bf16[256,1024]{0,1:T(8,128)(2,1)S(1)} all-gather(bf16[256,128]{0,1:T(8,128)(2,1)S(1)} %convert_element_type.12), channel_id=1, replica_groups=mesh['fsdp'=32,'tp'=8] {'tp'}, dimensions={1}, use_global_device_ids=true | all-gather | bytes 589824 | tf_op jit(solution)/shard_map/all_gather | solution.py:23
  254.4 0.0 copy-done
  254.4 7.3 %fusion.5 = f32[1024,3584]{1,0:T(8,128)} fusion(bf16[256,1024]{0,1:T(8,128)(2,1)S(1)} %all_gather.6, bf16[256,3584]{1,0:T(8,128)(2,1)S(1)} %copy-done), kind=kOutput, calls=%fused_computation.9 | convolution fusion | flops 1879048192 | bytes 17039360 | tf_op jit(solution)/shard_map/dot_general | solution.py:25
  261.6 0.0 copy-start.1
  261.6 0.0 copy-start.2
  261.6 0.0 reduce-scatter.5.cloned.1.call-update
  261.7 0.0 all-gather.2.cloned.1.call-start
  261.7 155.7 %reduce-scatter.5.cloned.1.call-done = f32[32,3584]{1,0:T(8,128)} async-done(((f32[1024,3584]{1,0:T(8,128)}), f32[32,3584]{1,0:T(8,128)}) %reduce-scatter.5.cloned.1.call-update) | async-done | bytes 458768 | tf_op jit(solution)/shard_map/reduce_scatter | solution.py:24
  417.4 0.0 copy-done.1
  417.4 0.0 copy-done.2
  417.4 2.2 divide_convert_fusion
  419.5 0.0 all-gather.2.cloned.1.call-update
  419.6 74.2 %all-gather.2.cloned.1.call-done = bf16[1024,3584]{1,0:T(8,128)(2,1)} async-done(((bf16[32,3584]{1,0:T(8,128)(2,1)}), bf16[1024,3584]{1,0:T(8,128)(2,1)}) %all-gather.2.cloned.1.call-update) | async-done | bytes 7340048 | tf_op jit(solution)/shard_map/all_gather | solution.py:39
  493.7 6.5 %fusion = bf16[256,3584]{0,1:T(8,128)(2,1)} fusion(bf16[1024,3584]{1,0:T(8,128)(2,1)} %all-gather.2.cloned.1.call-done, bf16[256,1024]{1,0:T(8,128)(2,1)S(1)} %copy-done.3), kind=kOutput, calls=%fused_computation.2 | convolution fusion | flops 1879965696 | bytes 9699328 | tf_op jit(solution)/shard_map/dot_general | solution.py:37
  500.2 3.8 copy.12
Async XLA Ops:
  7.2 247.2 %copy-start = (bf16[256,3584]{1,0:T(8,128)(2,1)S(1)}, bf16[256,3584]{1,0:T(8,128)(2,1)}, u32[]{:S(2)}) copy-start(bf16[256,3584]{1,0:T(8,128)(2,1)} %param.6) | copy-start | bytes 5505028
  13.8 108.5 %all-to-all-start = ((bf16[256,32,256]{0,2,1:T(8,128)(2,1)}), bf16[256,32,256]{0,2,1:T(8,128)(2,1)}, u32[]{:S(2)}, u32[]{:S(2)}) async-start(bf16[256,32,256]{0,2,1:T(8,128)(2,1)} %bitcast.12), calls=%async_computation | async-start | bytes 8388608 | tf_op jit(solution)/shard_map/all_to_all | solution.py:15
  26.4 202.9 %reduce-scatter.3.cloned.1.call-start = ((), (), s32[]{:S(2)}) async-start(), calls=%async_computation.3 | async-start | bytes 4325376 | tf_op jit(solution)/shard_map/reduce_scatter | solution.py:17
  122.3 6.5 %copy-start.3 = (bf16[256,1024]{1,0:T(8,128)(2,1)S(1)}, bf16[256,1024]{1,0:T(8,128)(2,1)}, u32[]{:S(2)}) copy-start(bf16[256,1024]{1,0:T(8,128)(2,1)} %param.7) | copy-start | bytes 1572868
  134.5 282.9 %reduce-scatter.5.cloned.1.call-start = ((), (), s32[]{:S(2)}) async-start(), calls=%async_computation.4 | async-start | bytes 15138816 | tf_op jit(solution)/shard_map/reduce_scatter | solution.py:24
  261.6 155.7 %copy-start.1 = (f32[32,3584]{1,0:T(8,128)S(1)}, f32[32,3584]{1,0:T(8,128)}, u32[]{:S(2)}) copy-start(f32[32,3584]{1,0:T(8,128)} %param.9) | copy-start | bytes 1376260
  261.6 155.7 %copy-start.2 = (f32[32,3584]{1,0:T(8,128)S(1)}, f32[32,3584]{1,0:T(8,128)}, u32[]{:S(2)}) copy-start(f32[32,3584]{1,0:T(8,128)} %param.8) | copy-start | bytes 1376260
  261.7 232.1 %all-gather.2.cloned.1.call-start = ((), (), s32[]{:S(2)}) async-start(), calls=%async_computation.5 | async-start | bytes 7569408 | tf_op jit(solution)/shard_map/all_gather | solution.py:39
Sparse Core Ops, SparseCore 0:
  134.6 94.6 reduce-scatter.2
  261.8 155.5 reduce-scatter.4
  420.5 73.1 all-gather.1
where the time goes:
time: 511 us
  waiting for transfers between devices  420 us (82%)
  blocking collectives  24.1 us (5%)
  matrix products  19.4 us (4%)
  local copies, waits for them, and re-layouts  16.9 us (3%)
  between operations  13.8 us (3%)
  starting transfers between devices  12.8 us (3%)
    reduce_scatter x1, waiting for transfers between devices, body(): lax.psum_scatter(lax.dot_general(coords, grad_output, (((0,), (0,)), ((),...  156 us
    all_to_all x1, waiting for transfers between devices, body(): lax.all_to_all(activations, 'fsdp', split_axis=1, concat_axis=0, tiled=True)  95.8 us
    reduce_scatter x1, waiting for transfers between devices, body(): lax.psum_scatter(jnp.dot(spread, proj_block, preferred_element_type=jnp.f...  94.8 us
    all_gather x1, waiting for transfers between devices, body(): lax.all_gather(direction, 'fsdp', axis=0, tiled=True)  74.2 us
    all_gather x1, blocking collectives, body(): coords = lax.all_gather(partial_coords, 'tp', axis=1, tiled=True)  24.1 us
    all_to_all x1, starting transfers between devices, body(): lax.all_to_all(activations, 'fsdp', split_axis=1, concat_axis=0, tiled=True)  12.6 us
    unnamed x10, local copies, waits for them, and re-layouts  10.4 us
  transfers between devices with their start and end apart: 4, of which 4 were waited for; matrix products, arithmetic and copies ran while one was open for 0% of the time, Pallas kernels for 0%

commit v1 on v0

--- a/solution.py
+++ b/solution.py
@@ -12,22 +12,17 @@
     tp_count = lax.axis_size("tp")
     tp_place = lax.axis_index("tp")
     column_count = rank_width // tp_count
-    spread = lax.all_to_all(activations, "fsdp", split_axis=1, concat_axis=0, tiled=True)
     proj_block = lax.dynamic_slice_in_dim(projector, tp_place * column_count, column_count, 1)
-    partial_coords = lax.psum_scatter(
-        jnp.dot(spread, proj_block, preferred_element_type=jnp.float32),
-        "fsdp",
-        scatter_dimension=0,
-        tiled=True,
+    proj_columns = lax.all_gather(proj_block, "fsdp", axis=0, tiled=True)
+    own_coords = jnp.dot(
+        activations, proj_columns, preferred_element_type=jnp.float32
     ).astype(jnp.bfloat16)
-    coords = lax.all_gather(partial_coords, "tp", axis=1, tiled=True)
-    lowrank = lax.psum_scatter(
-        lax.dot_general(
-            coords, grad_output, (((0,), (0,)), ((), ())), preferred_element_type=jnp.float32
-        ),
-        "fsdp",
-        scatter_dimension=0,
-        tiled=True,
+    coords = lax.all_gather(own_coords, "tp", axis=1, tiled=True)
+    partial = lax.dot_general(
+        coords, grad_output, (((0,), (0,)), ((), ())), preferred_element_type=jnp.float32
+    ).astype(jnp.bfloat16)
+    lowrank = lax.psum_scatter(partial, "fsdp", scatter_dimension=0, tiled=True).astype(
+        jnp.float32
     )
     new_first = 0.9 * first_moment + 0.1 * lowrank
     new_second = 0.99 * second_moment + 0.01 * lowrank * lowrank

time: 511 us -> 312 us (0.61)
  waiting for transfers between devices: 420 us -> 250 us
  starting transfers between devices: 12.8 us -> 0.12 us
  local copies, waits for them, and re-layouts: 16.9 us -> 5.42 us
    reduce_scatter x2 -> x1, waiting for transfers between devices: 250 us -> 116 us  [body(): lax.psum_scatter(partial, 'fsdp', scatter_dimension=0, tiled=True)]
    all_to_all x1 -> x0, waiting for transfers between devices: 95.8 us -> none  [body(): lax.all_to_all(activations, 'fsdp', split_axis=1, concat_axis=0, tiled=True)]
    all_gather x0 -> x1, waiting for transfers between devices: none -> 61.2 us  [body(): proj_columns = lax.all_gather(proj_block, 'fsdp', axis=0, tiled=True)]
    all_to_all x1 -> x0, starting transfers between devices: 12.6 us -> none  [body(): lax.all_to_all(activations, 'fsdp', split_axis=1, concat_axis=0, tiled=True)]
    unnamed x10 -> x9, local copies, waits for them, and re-layouts: 10.4 us -> 3.82 us
    all_to_all x1 -> x0, local copies, waits for them, and re-layouts: 6.51 us -> none  [body(): lax.all_to_all(activations, 'fsdp', split_axis=1, concat_axis=0, tiled=True)]
  transfers between devices with their start and end apart: 4 -> 3, of which waited for: 4 -> 3; matrix products, arithmetic and copies ran while one was open for 0% -> 0% of each run, Pallas kernels for 0% -> 0%
where the time goes in v1:
time: 312 us
  waiting for transfers between devices  250 us (80%)
  blocking collectives  24.4 us (8%)
  matrix products  15.9 us (5%)
  between operations  13.8 us (4%)
  local copies, waits for them, and re-layouts  5.42 us (2%)
    reduce_scatter x1, waiting for transfers between devices, body(): lax.psum_scatter(partial, 'fsdp', scatter_dimension=0, tiled=True)  116 us
    all_gather x1, waiting for transfers between devices, body(): lax.all_gather(direction, 'fsdp', axis=0, tiled=True)  73.2 us
    all_gather x1, waiting for transfers between devices, body(): proj_columns = lax.all_gather(proj_block, 'fsdp', axis=0, tiled=True)  61.2 us
    all_gather x1, blocking collectives, body(): coords = lax.all_gather(own_coords, 'tp', axis=1, tiled=True)  24.4 us
    dot_general x1, matrix products, body(): jnp.dot(projector, lax.all_gather(direction, 'fsdp', axis=0, tiled=True),...  6.5 us
  transfers between devices with their start and end apart: 3, of which 3 were waited for; matrix products, arithmetic and copies ran while one was open for 0% of the time, Pallas kernels for 0%

profile of v1, /device:TPU:1, one launch (start us, length us, event | category | flops | bytes accessed | tf_op | source)
XLA Modules:
  0.0 311.9 jit_solution(6757841526165121869)
XLA Ops:
  7.2 0.0 copy-start
  7.2 0.0 all-gather.3.cloned.1.call-start
  7.2 1.6 constant_dynamic-slice_fusion
  8.8 0.0 all-gather.3.cloned.1.call-update
  8.9 0.0 reduce-scatter.2.cloned.1.call-start
  8.9 61.2 %all-gather.3.cloned.1.call-done = bf16[8192,128]{1,0:T(8,128)(2,1)} async-done(((bf16[256,128]{1,0:T(8,128)(2,1)}), bf16[8192,128]{1,0:T(8,128)(2,1)}) %all-gather.3.cloned.1.call-update) | async-done | bytes 2097168 | tf_op jit(solution)/shard_map/all_gather | solution.py:16
  70.1 4.4 %fusion.1 = bf16[256,128]{0,1:T(8,128)(2,1)S(1)} fusion(bf16[8192,128]{1,0:T(8,128)(2,1)} %all-gather.3.cloned.1.call-done, bf16[256,8192]{1,0:T(8,128)(2,1)} %param.5), kind=kOutput, calls=%fused_computation.4 | convolution fusion | flops 536903680 | bytes 6356992 | tf_op jit(solution)/shard_map/dot_general | solution.py:17
  74.4 24.4 %all_gather.10 = bf16[256,1024]{0,1:T(8,128)(2,1)S(1)} all-gather(bf16[256,128]{0,1:T(8,128)(2,1)S(1)} %fusion.1), channel_id=1, replica_groups=mesh['fsdp'=32,'tp'=8] {'tp'}, dimensions={1}, use_global_device_ids=true | all-gather | bytes 589824 | tf_op jit(solution)/shard_map/all_gather | solution.py:20
  98.8 0.0 copy-done
  98.8 5.0 %convolution_convert_fusion = bf16[1024,3584]{1,0:T(8,128)(2,1)} fusion(bf16[256,1024]{0,1:T(8,128)(2,1)S(1)} %all_gather.10, bf16[256,3584]{1,0:T(8,128)(2,1)S(1)} %copy-done), kind=kOutput, calls=%fused_computation | convolution fusion | flops 1882718208 | bytes 9699328 | tf_op jit(solution)/shard_map/dot_general | solution.py:21
  103.8 0.0 copy-start.1
  103.9 0.0 copy-start.2
  103.9 0.0 copy-start.3
  103.9 0.0 reduce-scatter.2.cloned.1.call-update
  103.9 0.0 all-gather.5.cloned.1.call-start
  103.9 115.9 %reduce-scatter.2.cloned.1.call-done = bf16[32,3584]{1,0:T(8,128)(2,1)} async-done(((bf16[1024,3584]{1,0:T(8,128)(2,1)}), bf16[32,3584]{1,0:T(8,128)(2,1)}) %reduce-scatter.2.cloned.1.call-update) | async-done | bytes 229392 | tf_op jit(solution)/shard_map/reduce_scatter | solution.py:24
  219.8 0.0 copy-done.1
  219.8 0.0 copy-done.2
  219.8 2.1 divide_convert_fusion
  221.9 0.0 all-gather.5.cloned.1.call-update
  221.9 73.2 %all-gather.5.cloned.1.call-done = bf16[1024,3584]{1,0:T(8,128)(2,1)} async-done(((bf16[32,3584]{1,0:T(8,128)(2,1)}), bf16[1024,3584]{1,0:T(8,128)(2,1)}) %all-gather.5.cloned.1.call-update) | async-done | bytes 7340048 | tf_op jit(solution)/shard_map/all_gather | solution.py:34
  295.1 0.0 copy-done.3
  295.1 6.5 %fusion = bf16[256,3584]{0,1:T(8,128)(2,1)} fusion(bf16[1024,3584]{1,0:T(8,128)(2,1)} %all-gather.5.cloned.1.call-done, bf16[256,1024]{1,0:T(8,128)(2,1)S(1)} %copy-done.3), kind=kOutput, calls=%fused_computation.2 | convolution fusion | flops 1879965696 | bytes 9699328 | tf_op jit(solution)/shard_map/dot_general | solution.py:32
  301.6 3.8 %copy.8 = bf16[256,3584]{1,0:T(8,128)(2,1)} copy(bf16[256,3584]{0,1:T(8,128)(2,1)} %fusion) | data formatting | bytes 3670016
Async XLA Ops:
  7.2 91.7 %copy-start = (bf16[256,3584]{1,0:T(8,128)(2,1)S(1)}, bf16[256,3584]{1,0:T(8,128)(2,1)}, u32[]{:S(2)}) copy-start(bf16[256,3584]{1,0:T(8,128)(2,1)} %param.6) | copy-start | bytes 5505028
  7.2 62.9 %all-gather.3.cloned.1.call-start = ((), (), s32[]{:S(2)}) async-start(), calls=%async_computation.1 | async-start | bytes 2162688 | tf_op jit(solution)/shard_map/all_gather | solution.py:16
  8.9 211.0 %reduce-scatter.2.cloned.1.call-start = ((), (), s32[]{:S(2)}) async-start(), calls=%async_computation.2 | async-start | bytes 7569408 | tf_op jit(solution)/shard_map/reduce_scatter | solution.py:24
  103.8 116.0 %copy-start.1 = (f32[32,3584]{1,0:T(8,128)S(1)}, f32[32,3584]{1,0:T(8,128)}, u32[]{:S(2)}) copy-start(f32[32,3584]{1,0:T(8,128)} %param.9) | copy-start | bytes 1376260
  103.9 116.0 %copy-start.2 = (f32[32,3584]{1,0:T(8,128)S(1)}, f32[32,3584]{1,0:T(8,128)}, u32[]{:S(2)}) copy-start(f32[32,3584]{1,0:T(8,128)} %param.8) | copy-start | bytes 1376260
  103.9 191.2 %copy-start.3 = (bf16[256,1024]{1,0:T(8,128)(2,1)S(1)}, bf16[256,1024]{1,0:T(8,128)(2,1)}, u32[]{:S(2)}) copy-start(bf16[256,1024]{1,0:T(8,128)(2,1)} %param.7) | copy-start | bytes 1572868
  103.9 191.2 %all-gather.5.cloned.1.call-start = ((), (), s32[]{:S(2)}) async-start(), calls=%async_computation.3 | async-start | bytes 7569408 | tf_op jit(solution)/shard_map/all_gather | solution.py:34
Sparse Core Ops, SparseCore 0:
  11.1 58.8 all-gather.2
  104.0 115.7 reduce-scatter.1
  223.3 71.7 all-gather.4
